TPU v7x, 32 devices: a whole 2x2x4 slice. The times are simulated.
32 devices in a mesh: dp: 8 (over y, x, core), tensor: 4 (over z).
Axes of the slice: x: 2, y: 2, z: 4, core: 2. Of those that a mesh axis runs over, the one named last changes fastest.
Arguments:
- hidden: bfloat16 [1024, 8192], P('dp', 'tensor')
- rotation: float32 [8192, 8192], P('dp', 'tensor'), may hold values from -0.0625 to 0.0625
- channel_scale: float32 [8192], P('tensor')
- lengths: int32 [16], P('dp'), may hold values from 16 to 64, as said below
Outputs:
- direction: float32 [8192, 8192], P('dp', 'tensor')
- loss: float32 [], replicated
Inputs may be any that keep to these rules, and one draw needn't show every extreme that they name: `lengths`: each sequence's valid length; some sequence is full in every draw.
All inputs are finite; a program needn't handle non-finite values.
Results may differ from a plain program's by a relative error of at most 0.00075.
The roundings to bfloat16 on the way count: a program that leaves them out, or rounds other values in their place, can miss the bound.
Values may be sent and summed in bfloat16 or wider, within the bound.
A program may use at most 128 MiB of HBM per device.

v0:
```python
import math
import jax
import jax.numpy as jnp
from jax import lax
from jax.sharding import PartitionSpec as P

D = 8192
SEQ = 64


def local(hidden, rotation, channel_scale, lengths):
    narrow_rotation = rotation.astype(jnp.bfloat16)
    features = lax.all_gather(hidden, "tensor", axis=1, tiled=True)
    column_blocks = lax.all_to_all(features, "dp", split_axis=1, concat_axis=0, tiled=True)
    partial = jnp.dot(column_blocks, narrow_rotation, preferred_element_type=jnp.float32)
    rotated = lax.psum_scatter(partial, "dp", scatter_dimension=0, tiled=True)
    scaled = rotated * channel_scale[None, :]
    token_square = lax.psum(jnp.sum(scaled * scaled, axis=1), "tensor")
    step_size = 4.0 * jnp.sqrt(token_square / D + 1e-06)[:, None]
    token_index = jnp.arange(hidden.shape[0], dtype=jnp.int32)
    position = token_index % SEQ
    sequence_index = token_index // SEQ
    sequence_count = lengths.shape[0]
    owners = sequence_index[:, None] == jnp.arange(sequence_count, dtype=jnp.int32)[None, :]
    inside = position[:, None] < lengths[None, :]
    live_mask = jnp.sum(jnp.where(owners & inside, 1.0, 0.0), axis=1).astype(jnp.float32)[:, None]
    angles = math.pi * scaled / step_size
    error_local = jnp.sum(live_mask * jnp.sin(angles) ** 2)
    count_local = jnp.sum(lengths).astype(jnp.float32) / lax.axis_size("tensor")
    error_slope = (
        live_mask * (math.pi / step_size) * jnp.sin(2.0 * angles) * channel_scale[None, :]
    ).astype(jnp.bfloat16)
    gradient = lax.dot_general(
        column_blocks,
        lax.all_gather(error_slope, "dp", axis=0, tiled=True),
        (((0,), (0,)), ((), ())),
        preferred_element_type=jnp.float32,
    )
    error_sum, count = lax.psum((error_local, count_local), ("dp", "tensor"))
    grad_square = lax.psum(jnp.sum(gradient * gradient), ("dp", "tensor"))
    direction = gradient / jnp.sqrt(grad_square / (D * D) + 1e-06)
    loss = error_sum / (D * count)
    return (direction, loss)


def solution(mesh):
    return jax.shard_map(
        local,
        mesh=mesh,
        in_specs=(P("dp", "tensor"), P("dp", "tensor"), P("tensor"), P("dp")),
        out_specs=(P("dp", "tensor"), P()),
        check_vma=False,
    )
```

profile of v0, /device:TPU:0, one launch (start us, length us, event | category | flops | bytes accessed | tf_op | source)
XLA Modules:
  0.0 305.9 jit_solution(8076852472374651479)
XLA Ops:
  7.2 0.0 all-gather.3.cloned.1.call-start
  7.2 2.0 copy.11
  9.3 0.0 all-gather.3.cloned.1.call-update
  9.3 0.0 reduce-scatter.2.cloned.1.call-start
  9.3 49.5 %all-gather.3.cloned.1.call-done = bf16[128,8192]{0,1:T(8,128)(2,1)} async-done(((bf16[128,2048]{0,1:T(8,128)(2,1)}), bf16[128,8192]{0,1:T(8,128)(2,1)}) %all-gather.3.cloned.1.call-update) | async-done | bytes 2097168 | tf_op jit(solution)/shard_map/all_gather | solution.py:13
  58.8 30.2 %all_to_all.19 = bf16[128,8,1024]{0,2,1:T(8,128)(2,1)S(1)} all-to-all(bf16[128,8,1024]{0,2,1:T(8,128)(2,1)} %bitcast.11), channel_id=1, replica_groups=mesh['dp'=8,'tensor'=4] {'dp'}, dimensions={1} | all-to-all | bytes 4194304 | tf_op jit(solution)/shard_map/all_to_all | solution.py:14
  89.0 2.6 copy.12
  91.6 11.9 %fusion = f32[1024,2048]{1,0:T(8,128)} fusion(bf16[1024,1024]{1,0:T(8,128)(2,1)} %bitcast.9, f32[1024,2048]{1,0:T(8,128)} %param.5), kind=kOutput, calls=%fused_computation.2 | convolution fusion | flops 4297064448 | bytes 18874368 | tf_op jit(solution)/shard_map/dot_general | solution.py:15
  103.6 0.0 copy-start.2
  103.6 0.0 copy-start.1
  103.6 0.0 copy-start
  103.6 0.0 reduce-scatter.2.cloned.1.call-update
  103.6 0.0 all-gather.5.cloned.1.call-start
  103.6 0.6 copy-done.2
  104.2 0.1 fusion.2
  104.3 67.6 %reduce-scatter.2.cloned.1.call-done = f32[128,2048]{1,0:T(8,128)} async-done(((f32[1024,2048]{1,0:T(8,128)}), f32[128,2048]{1,0:T(8,128)}) %reduce-scatter.2.cloned.1.call-update) | async-done | bytes 1048592 | tf_op jit(solution)/shard_map/reduce_scatter | solution.py:16
  171.9 0.0 copy-done.1
  171.9 1.4 multiply_reduce_fusion.2
  173.3 11.7 %psum.28 = f32[128]{0:T(128)S(1)} all-reduce(f32[128]{0:T(128)S(1)} %multiply_reduce_fusion.2), channel_id=1, replica_groups=mesh['dp'=8,'tensor'=4] {'tensor'}, use_global_device_ids=true, to_apply=%region_3.4 | all-reduce | flops 128 | bytes 1024 | tf_op jit(solution)/shard_map/psum | solution.py:18
  185.0 9.9 %multiply_reduce_fusion.1 = (f32[]{:T(128)}, bf16[128,2048]{1,0:T(8,128)(2,1)}) fusion(f32[128]{0:T(128)S(1)} %fusion.2, f32[128]{0:T(128)S(1)} %get-tuple-element.15, f32[128,2048]{1,0:T(8,128)} %reduce-scatter.2.cloned.1.call-done, f32[2048]{0:T(1024)S(1)} %copy-done.1, f32[128]{0:T(128)S(1)} %get-tuple-element.16), kind=kLoop, calls=%fused_computation.4 | loop fusion | flops 2621439 | bytes 1582596 | tf_op jit(solution)/shard_map/reduce_sum | solution.py:28
  194.9 0.0 all-gather.5.cloned.1.call-update
  195.0 0.6 reduce_sum.49
  196.2 32.9 %all-gather.5.cloned.1.call-done = bf16[1024,2048]{1,0:T(8,128)(2,1)} async-done(((bf16[128,2048]{1,0:T(8,128)(2,1)}), bf16[1024,2048]{1,0:T(8,128)(2,1)}) %all-gather.5.cloned.1.call-update) | async-done | bytes 4194320 | tf_op jit(solution)/shard_map/all_gather | solution.py:35
  229.0 0.0 copy-done
  229.1 10.1 %multiply_reduce_fusion = (f32[]{:T(128)}, f32[2048,1024]{1,0:T(8,128)}) fusion(bf16[1024,2048]{1,0:T(8,128)(2,1)} %all-gather.5.cloned.1.call-done, bf16[1024,1024]{1,0:T(8,128)(2,1)S(1)} %bitcast.10), kind=kOutput, calls=%fused_computation.1 | convolution fusion | flops 4299161600 | bytes 14680068 | tf_op jit(solution)/shard_map/dot_general | solution.py:33
  239.2 39.6 %all-reduce = (f32[]{:T(128)}, f32[]{:T(128)}, f32[]{:T(128)}) all-reduce(f32[]{:T(128)} %get-tuple-element.17, f32[]{:T(128)} %get-tuple-element.13, f32[]{:T(128)S(6)} %div.59), channel_id=1, replica_groups=mesh['dp'=8,'tensor'=4] {'dp','tensor'}, use_global_device_ids=true, to_apply=%region_5.6 | all-reduce | flops 3 | bytes 24 | tf_op jit(solution)/shard_map/psum | solution.py:40
  279.4 8.5 %divide_bitcast_fusion = f32[1024,2048]{0,1:T(8,128)} fusion(f32[2048,1024]{1,0:T(8,128)} %get-tuple-element.18, f32[]{:T(128)S(6)} %sqrt.7), kind=kLoop, calls=%fused_computation | loop fusion | flops 2097152 | bytes 16777220 | tf_op jit(solution)/shard_map/div | solution.py:41
  287.9 9.1 %copy.13 = f32[1024,2048]{1,0:T(8,128)} copy(f32[1024,2048]{0,1:T(8,128)} %divide_bitcast_fusion) | data formatting | bytes 16777216
  (2 shorter events, 0.0 us)
Async XLA Ops:
  7.2 51.6 %all-gather.3.cloned.1.call-start = ((), (), s32[]{:S(2)}) async-start(), calls=%async_computation.2 | async-start | bytes 2621440 | tf_op jit(solution)/shard_map/all_gather | solution.py:13
  9.3 162.6 %reduce-scatter.2.cloned.1.call-start = ((), (), s32[]{:S(2)}) async-start(), calls=%async_computation.3 | async-start | bytes 9437184 | tf_op jit(solution)/shard_map/reduce_scatter | solution.py:16
  103.6 0.7 copy-start.2
  103.6 68.4 %copy-start.1 = (f32[2048]{0:T(1024)S(1)}, f32[2048]{0:T(1024)}, u32[]{:S(2)}) copy-start(f32[2048]{0:T(1024)} %param.6) | copy-start | bytes 24580
  103.6 125.5 %copy-start = (bf16[8,128,1024]{2,1,0:T(8,128)(2,1)S(1)}, bf16[8,128,1024]{2,1,0:T(8,128)(2,1)}, u32[]{:S(2)}) copy-start(bf16[8,128,1024]{2,1,0:T(8,128)(2,1)} %copy.12) | copy-start | bytes 6291460
  103.6 125.5 %all-gather.5.cloned.1.call-start = ((), (), s32[]{:S(2)}) async-start(), calls=%async_computation.4 | async-start | bytes 4718592 | tf_op jit(solution)/shard_map/all_gather | solution.py:35
Sparse Core Ops, SparseCore 0:
  10.1 48.6 all-gather.2
  103.7 68.1 reduce-scatter.1
  195.1 33.9 all-gather.4
where the time goes:
time: 307 us; the launch traced here: 306 us
  waiting for transfers between devices  150 us (49%)
  blocking collectives  81.5 us (27%)
  matrix products  22 us (7%)
  other arithmetic  20.6 us (7%)
  between operations  17.3 us (6%)
  local copies, waits for them, and re-layouts  14.3 us (5%)
    reduce_scatter x1, waiting for transfers between devices, local(): rotated = lax.psum_scatter(partial, 'dp', scatter_dimension=0, tiled=True)  67.6 us
    all_gather x1, waiting for transfers between devices, local(): features = lax.all_gather(hidden, 'tensor', axis=1, tiled=True)  49.5 us
    psum x1, blocking collectives, local(): grad_square = lax.psum(jnp.sum(gradient * gradient), ('dp', 'tensor'))  39.6 us
    all_gather x1, waiting for transfers between devices, local(): lax.all_gather(error_slope, 'dp', axis=0, tiled=True)  32.9 us
    all_to_all x1, blocking collectives, local(): lax.all_to_all(features, 'dp', split_axis=1, concat_axis=0, tiled=True)  30.2 us
    dot_general x1, matrix products, local(): jnp.dot(column_blocks, narrow_rotation, preferred_element_type=jnp.float32)  11.9 us
    unnamed x8, local copies, waits for them, and re-layouts  11.7 us
    psum x1, blocking collectives, local(): token_square = lax.psum(jnp.sum(scaled * scaled, axis=1), 'tensor')  11.7 us
  transfers between devices with their start and end apart: 3, of which 3 were waited for; matrix products, arithmetic and copies ran while one was open for 0% of the time, Pallas kernels for 0%

commit v1 on v0

--- a/solution.py
+++ b/solution.py
@@ -8,9 +8,19 @@
 SEQ = 64
 
 
+def pass_along(block, axis, dim):
+    size = lax.axis_size(axis)
+    held, pieces = (block, [block])
+    for _ in range(size - 1):
+        held = lax.ppermute(held, axis, [(i, (i + 1) % size) for i in range(size)])
+        pieces.insert(0, held)
+    flat = jnp.concatenate(pieces, axis=dim)
+    return jnp.roll(flat, (lax.axis_index(axis) + 1) * block.shape[dim], axis=dim)
+
+
 def local(hidden, rotation, channel_scale, lengths):
     narrow_rotation = rotation.astype(jnp.bfloat16)
-    features = lax.all_gather(hidden, "tensor", axis=1, tiled=True)
+    features = pass_along(hidden, "tensor", 1)
     column_blocks = lax.all_to_all(features, "dp", split_axis=1, concat_axis=0, tiled=True)
     partial = jnp.dot(column_blocks, narrow_rotation, preferred_element_type=jnp.float32)
     rotated = lax.psum_scatter(partial, "dp", scatter_dimension=0, tiled=True)

time: 307 us -> 293 us (0.954)
  local copies, waits for them, and re-layouts: 14.3 us -> 5.15 us
  waiting for transfers between devices: 150 us -> 143 us
    all_gather x1 -> x0, waiting for transfers between devices: 49.5 us -> none  [local(): features = lax.all_gather(hidden, 'tensor', axis=1, tiled=True)]
    ppermute x0 -> x3, waiting for transfers between devices: none -> 42.8 us  [pass_along(): held = lax.ppermute(held, axis, [(i, (i + 1) % size) for i in range(size)])]
    unnamed x8 -> x14, local copies, waits for them, and re-layouts: 11.7 us -> 2.34 us
    ppermute x0 -> x3, starting transfers between devices: none -> 3.08 us  [pass_along(): held = lax.ppermute(held, axis, [(i, (i + 1) % size) for i in range(size)])]
  transfers between devices with their start and end apart: 3 -> 5, of which waited for: 3 -> 5; matrix products, arithmetic and copies ran while one was open for 0% -> 0% of each run, Pallas kernels for 0% -> 0%
where the time goes in v1:
time: 293 us; the launch traced here: 292 us
  waiting for transfers between devices  143 us (49%)
  blocking collectives  80.9 us (28%)
  matrix products  22.1 us (8%)
  other arithmetic  20.5 us (7%)
  between operations  17.8 us (6%)
  local copies, waits for them, and re-layouts  5.15 us (2%)
  starting transfers between devices  3.16 us (1%)
    reduce_scatter x1, waiting for transfers between devices, local(): rotated = lax.psum_scatter(partial, 'dp', scatter_dimension=0, tiled=True)  67.1 us
    ppermute x3, waiting for transfers between devices, pass_along(): held = lax.ppermute(held, axis, [(i, (i + 1) % size) for i in range(size)])  42.8 us
    psum x1, blocking collectives, local(): grad_square = lax.psum(jnp.sum(gradient * gradient), ('dp', 'tensor'))  39.6 us
    all_gather x1, waiting for transfers between devices, local(): lax.all_gather(error_slope, 'dp', axis=0, tiled=True)  32.9 us
    all_to_all x1, blocking collectives, local(): lax.all_to_all(features, 'dp', split_axis=1, concat_axis=0, tiled=True)  29.6 us
    dot_general x1, matrix products, local(): jnp.dot(column_blocks, narrow_rotation, preferred_element_type=jnp.float32)  11.9 us
    psum x1, blocking collectives, local(): token_square = lax.psum(jnp.sum(scaled * scaled, axis=1), 'tensor')  11.7 us
    dot_general x1, matrix products, local(): lax.dot_general(column_blocks, lax.all_gather(error_slope, 'dp', axis=0,...  10.2 us
  transfers between devices with their start and end apart: 5, of which 5 were waited for; matrix products, arithmetic and copies ran while one was open for 0% of the time, Pallas kernels for 0%

profile of v1, /device:TPU:0, one launch (start us, length us, event | category | flops | bytes accessed | tf_op | source)
XLA Modules:
  0.0 292.4 jit_solution(8945472084123297363)
XLA Ops:
  7.2 0.0 reduce-scatter.2.cloned.1.call-start
  7.2 1.3 copy.10
  8.5 3.1 %collective-permute-start = (bf16[128,2048]{0,1:T(8,128)(2,1)S(1)}, bf16[128,2048]{0,1:T(8,128)(2,1)S(1)}, u32[]{:S(2)}, u32[]{:S(2)}) collective-permute-start(bf16[128,2048]{0,1:T(8,128)(2,1)S(1)} %copy.10), channel_id=1, source_target_pairs={{0,1},{1,2},{2,3},{3,0},{4,5},{5,6},{6,7},{7,4},{8,9},{9,10},{10,1... | collective-permute-start | bytes 1572872 | tf_op jit(solution)/shard_map/ppermute | solution.py:15
  11.6 13.9 %collective-permute-done = bf16[128,2048]{0,1:T(8,128)(2,1)S(1)} collective-permute-done((bf16[128,2048]{0,1:T(8,128)(2,1)S(1)}, bf16[128,2048]{0,1:T(8,128)(2,1)S(1)}, u32[]{:S(2)}, u32[]{:S(2)}) %collective-permute-start) | collective-permute-done | bytes 524320 | tf_op jit(solution)/shard_map/ppermute | solution.py:15
  25.6 0.0 collective-permute-start.1
  25.6 14.9 %collective-permute-done.1 = bf16[128,2048]{0,1:T(8,128)(2,1)S(1)} collective-permute-done((bf16[128,2048]{0,1:T(8,128)(2,1)S(1)}, bf16[128,2048]{0,1:T(8,128)(2,1)S(1)}, u32[]{:S(2)}, u32[]{:S(2)}) %collective-permute-start.1) | collective-permute-done | bytes 524320 | tf_op jit(solution)/shard_map/ppermute | solution.py:15
  40.5 0.0 collective-permute-start.2
  40.5 14.0 %collective-permute-done.2 = bf16[128,2048]{0,1:T(8,128)(2,1)S(1)} collective-permute-done((bf16[128,2048]{0,1:T(8,128)(2,1)S(1)}, bf16[128,2048]{0,1:T(8,128)(2,1)S(1)}, u32[]{:S(2)}, u32[]{:S(2)}) %collective-permute-start.2) | collective-permute-done | bytes 524320 | tf_op jit(solution)/shard_map/ppermute | solution.py:15
  54.5 0.1 constant_dynamic-update-slice_fusion.6
  54.6 0.1 constant_dynamic-update-slice_fusion.5
  54.6 0.1 constant_dynamic-update-slice_fusion.4
  54.7 0.1 constant_dynamic-update-slice_fusion.3
  54.8 0.1 constant_dynamic-update-slice_fusion.2
  54.9 0.1 constant_dynamic-update-slice_fusion.1
  55.0 0.1 constant_dynamic-update-slice_fusion
  55.0 0.1 constant_dynamic-slice_fusion
  55.2 29.6 %all_to_all.19 = bf16[128,8,1024]{0,2,1:T(8,128)(2,1)S(1)} all-to-all(bf16[128,8,1024]{0,2,1:T(8,128)(2,1)S(1)} %bitcast.6), channel_id=1, replica_groups=mesh['dp'=8,'tensor'=4] {'dp'}, dimensions={1} | all-to-all | bytes 4194304 | tf_op jit(solution)/shard_map/all_to_all | solution.py:24
  84.8 2.6 copy.13
  87.4 11.9 %fusion = f32[1024,2048]{1,0:T(8,128)} fusion(bf16[1024,1024]{1,0:T(8,128)(2,1)} %bitcast.8, f32[1024,2048]{1,0:T(8,128)} %param.5), kind=kOutput, calls=%fused_computation.2 | convolution fusion | flops 4297064448 | bytes 18874368 | tf_op jit(solution)/shard_map/dot_general | solution.py:25
  99.3 0.0 copy-start.2
  99.3 0.0 copy-start.1
  99.3 0.0 copy-start
  99.3 0.0 reduce-scatter.2.cloned.1.call-update
  99.4 0.0 all-gather.2.cloned.1.call-start
  99.4 0.6 copy-done.2
  100.0 0.1 fusion.2
  100.1 67.1 %reduce-scatter.2.cloned.1.call-done = f32[128,2048]{1,0:T(8,128)} async-done(((f32[1024,2048]{1,0:T(8,128)}), f32[128,2048]{1,0:T(8,128)}) %reduce-scatter.2.cloned.1.call-update) | async-done | bytes 1048592 | tf_op jit(solution)/shard_map/reduce_scatter | solution.py:26
  167.1 0.0 copy-done.1
  167.1 1.4 multiply_reduce_fusion.2
  168.5 11.7 %psum.28 = f32[128]{0:T(128)S(1)} all-reduce(f32[128]{0:T(128)S(1)} %multiply_reduce_fusion.2), channel_id=1, replica_groups=mesh['dp'=8,'tensor'=4] {'tensor'}, use_global_device_ids=true, to_apply=%region_3.4 | all-reduce | flops 128 | bytes 1024 | tf_op jit(solution)/shard_map/psum | solution.py:28
  180.2 9.9 %multiply_reduce_fusion.1 = (f32[]{:T(128)}, bf16[128,2048]{1,0:T(8,128)(2,1)}) fusion(f32[128]{0:T(128)S(1)} %fusion.2, f32[128]{0:T(128)S(1)} %get-tuple-element.7, f32[128,2048]{1,0:T(8,128)} %reduce-scatter.2.cloned.1.call-done, f32[2048]{0:T(1024)S(1)} %copy-done.1, f32[128]{0:T(128)S(1)} %get-tuple-element.8), kind=kLoop, calls=%fused_computation.4 | loop fusion | flops 2621439 | bytes 1582596 | tf_op jit(solution)/shard_map/reduce_sum | solution.py:38
  190.1 0.0 all-gather.2.cloned.1.call-update
  190.2 0.6 reduce_sum.49
  191.4 32.9 %all-gather.2.cloned.1.call-done = bf16[1024,2048]{1,0:T(8,128)(2,1)} async-done(((bf16[128,2048]{1,0:T(8,128)(2,1)}), bf16[1024,2048]{1,0:T(8,128)(2,1)}) %all-gather.2.cloned.1.call-update) | async-done | bytes 4194320 | tf_op jit(solution)/shard_map/all_gather | solution.py:45
  224.3 0.0 copy-done
  224.3 10.2 %multiply_reduce_fusion = (f32[]{:T(128)}, f32[1024,2048]{1,0:T(8,128)}) fusion(bf16[1024,1024]{1,0:T(8,128)(2,1)S(1)} %bitcast.9, bf16[1024,2048]{1,0:T(8,128)(2,1)} %all-gather.2.cloned.1.call-done), kind=kOutput, calls=%fused_computation | convolution fusion | flops 4299161600 | bytes 14680068 | tf_op jit(solution)/shard_map/dot_general | solution.py:43
  234.5 39.6 %all-reduce = (f32[]{:T(128)}, f32[]{:T(128)}, f32[]{:T(128)}) all-reduce(f32[]{:T(128)} %get-tuple-element.9, f32[]{:T(128)} %get-tuple-element.5, f32[]{:T(128)S(6)} %div.55), channel_id=1, replica_groups=mesh['dp'=8,'tensor'=4] {'dp','tensor'}, use_global_device_ids=true, to_apply=%region_5.6 | all-reduce | flops 3 | bytes 24 | tf_op jit(solution)/shard_map/psum | solution.py:50
  276.0 8.4 %broadcast_divide_fusion = f32[1024,2048]{1,0:T(8,128)} fusion(f32[1024,2048]{1,0:T(8,128)} %get-tuple-element.10, f32[]{:T(128)S(6)} %sqrt.7), kind=kLoop, calls=%fused_computation.1 | loop fusion | flops 2097152 | bytes 16777220 | tf_op jit(solution)/shard_map/div | solution.py:51
  (3 shorter events, 0.1 us)
Async XLA Ops:
  7.2 160.0 %reduce-scatter.2.cloned.1.call-start = ((), (), s32[]{:S(2)}) async-start(), calls=%async_computation.2 | async-start | bytes 9437184 | tf_op jit(solution)/shard_map/reduce_scatter | solution.py:26
  8.5 17.0 %collective-permute-start = (bf16[128,2048]{0,1:T(8,128)(2,1)S(1)}, bf16[128,2048]{0,1:T(8,128)(2,1)S(1)}, u32[]{:S(2)}, u32[]{:S(2)}) collective-permute-start(bf16[128,2048]{0,1:T(8,128)(2,1)S(1)} %copy.10), channel_id=1, source_target_pairs={{0,1},{1,2},{2,3},{3,0},{4,5},{5,6},{6,7},{7,4},{8,9},{9,10},{10,1... | collective-permute-start | bytes 1572872 | tf_op jit(solution)/shard_map/ppermute | solution.py:15
  25.6 14.9 %collective-permute-start.1 = (bf16[128,2048]{0,1:T(8,128)(2,1)S(1)}, bf16[128,2048]{0,1:T(8,128)(2,1)S(1)}, u32[]{:S(2)}, u32[]{:S(2)}) collective-permute-start(bf16[128,2048]{0,1:T(8,128)(2,1)S(1)} %collective-permute-done), channel_id=1, source_target_pairs={{0,1},{1,2},{2,3},{3,0},{4,5},{5,6},{6,7},{7,4},{8,9},{9,10},{10,1... | collective-permute-start | bytes 1572872 | tf_op jit(solution)/shard_map/ppermute | solution.py:15
  40.5 14.0 %collective-permute-start.2 = (bf16[128,2048]{0,1:T(8,128)(2,1)S(1)}, bf16[128,2048]{0,1:T(8,128)(2,1)S(1)}, u32[]{:S(2)}, u32[]{:S(2)}) collective-permute-start(bf16[128,2048]{0,1:T(8,128)(2,1)S(1)} %collective-permute-done.1), channel_id=1, source_target_pairs={{0,1},{1,2},{2,3},{3,0},{4,5},{5,6},{6,7},{7,4},{8,9},{9,10},{10,1... | collective-permute-start | bytes 1572872 | tf_op jit(solution)/shard_map/ppermute | solution.py:15
  99.3 0.7 copy-start.2
  99.3 67.8 %copy-start.1 = (f32[2048]{0:T(1024)S(1)}, f32[2048]{0:T(1024)}, u32[]{:S(2)}) copy-start(f32[2048]{0:T(1024)} %param.6) | copy-start | bytes 24580
  99.3 124.9 %copy-start = (bf16[8,128,1024]{2,1,0:T(8,128)(2,1)S(1)}, bf16[8,128,1024]{2,1,0:T(8,128)(2,1)}, u32[]{:S(2)}) copy-start(bf16[8,128,1024]{2,1,0:T(8,128)(2,1)} %copy.13) | copy-start | bytes 6291460
  99.4 124.9 %all-gather.2.cloned.1.call-start = ((), (), s32[]{:S(2)}) async-start(), calls=%async_computation.3 | async-start | bytes 4718592 | tf_op jit(solution)/shard_map/all_gather | solution.py:45
Sparse Core Ops, SparseCore 0:
  99.5 67.6 reduce-scatter.1
  190.3 33.9 all-gather.1
